TPU v7x, 32 devices: a whole 2x2x4 slice. The times are simulated.
32 devices in a mesh: mem: 32 (over z, y, x, core).
Axes of the slice: x: 2, y: 2, z: 4, core: 2. Of those that a mesh axis runs over, the one named last changes fastest.
Arguments:
- query_feats: float32 [32768, 8], P('mem'), may hold values from -6 to 6
- feature_mask: int32 [32768, 8], P('mem'), may hold values from 0 to 1, as said below
- query_task: int32 [32768], P('mem'), may hold values from 0 to 3
- target_class: int32 [32768], P('mem'), may hold values from 0 to 15
- target_mask: int32 [32768], P('mem'), may hold values from 0 to 1, as said below
- memory_feats: float32 [2048, 8], P('mem'), may hold values from -6 to 6
- memory_task: int32 [2048], replicated, may hold values from 0 to 3, as said below
- memory_mask: int32 [2048], replicated, may hold values from 0 to 1, as said below
- anneal: float32 [1], replicated, may hold values from 0.3 to 0.7
- w_qkv: float32 [196608], P('mem'), may hold values from -0.375 to 0.375
- w_out: float32 [65536], P('mem'), may hold values from -6 to 6
- w_heads: float32 [6144], P('mem'), may hold values from -0.375 to 0.375
- w_small: float32 [1056], P('mem'), may hold values from 0.1 to 1.9
- m_qkv: float32 [196608], P('mem'), may hold values from -0.00015258789 to 0.00015258789
- m_out: float32 [65536], P('mem'), may hold values from -0.00015258789 to 0.00015258789
- m_heads: float32 [6144], P('mem'), may hold values from -0.00015258789 to 0.00015258789
- m_small: float32 [1056], P('mem'), may hold values from -0.00061035156 to 0.00061035156
- v_qkv: float32 [196608], P('mem'), may hold values from 9.536743e-12 to 3.814697e-11
- v_out: float32 [65536], P('mem'), may hold values from 9.536743e-13 to 3.8146973e-12
- v_heads: float32 [6144], P('mem'), may hold values from 9.536743e-12 to 3.814697e-11
- v_small: float32 [1056], P('mem'), may hold values from 1.5258789e-10 to 6.1035155e-10
Outputs:
- new_qkv: float32 [196608], P('mem')
- new_out: float32 [65536], P('mem')
- new_heads: float32 [6144], P('mem')
- new_small: float32 [1056], P('mem')
- first_qkv: float32 [196608], P('mem')
- first_out: float32 [65536], P('mem')
- first_heads: float32 [6144], P('mem')
- first_small: float32 [1056], P('mem')
- second_qkv: float32 [196608], P('mem')
- second_out: float32 [65536], P('mem')
- second_heads: float32 [6144], P('mem')
- second_small: float32 [1056], P('mem')
- copy_qkv: bfloat16 [196608], P('mem')
- copy_out: bfloat16 [65536], P('mem')
- copy_heads: bfloat16 [6144], P('mem')
- copy_small: bfloat16 [1056], P('mem')
- loss_value: float32 [1], replicated
- grad_norm: float32 [1], replicated
Inputs may be any that keep to these rules, and one draw needn't show every extreme that they name: `memory_mask`: the live rows of each device's 64 memory rows are a prefix of a quarter of them or more; the first device's rows are all live. `memory_task`: the first 4 memory rows have the tasks 0 to 3 in order. `target_mask`: the share of labelled queries rises along the query rows from about a quarter to about three quarters. `feature_mask`: the share of hidden features rises along the query rows from about a quarter to about three quarters.
All inputs are finite; a program needn't handle non-finite values.
Results may differ from a plain program's by a relative error of at most 0.0087.
Values may be sent and summed in bfloat16 or wider, within the bound.
A program may use at most 128 MiB of HBM per device.

v0:
```python
import math
import jax
import jax.numpy as jnp
from jax import lax
from jax.sharding import PartitionSpec as P

F = 8
D = 256
H = 8
C = 16
STEP = 10
eps_norm = 1e-05
max_norm = 0.05
beta_one = 0.9
beta_two = 0.999
adam_eps = 1e-08
decay_rate = 0.01
learn_rates = (0.05, 1.0, 0.05, 0.5)
masked_score = -1e30


def embed(feature_rows, table_flat, emb_bias):
    emb_table = table_flat.reshape(feature_rows.shape[1], -1)
    return (feature_rows[:, :, None] * emb_table[None]).reshape(
        feature_rows.shape[0], -1
    ) + emb_bias


def standard(hidden):
    centred = hidden - jnp.mean(hidden, -1, keepdims=True)
    inverse = lax.rsqrt(jnp.mean(centred * centred, -1, keepdims=True) + eps_norm)
    return (centred * inverse, inverse)


def norm_back(grad_out, hidden, gain_vec):
    normed, inverse = standard(hidden)
    grad_gain = jnp.sum(grad_out * normed, 0)
    grad_scaled = grad_out * gain_vec
    grad_hidden = inverse * (
        grad_scaled
        - jnp.mean(grad_scaled, -1, keepdims=True)
        - normed * jnp.mean(grad_scaled * normed, -1, keepdims=True)
    )
    return (grad_hidden, grad_gain)


def split_pair(values):
    upper = values.astype(jnp.bfloat16)
    lower = (values - upper.astype(jnp.float32)).astype(jnp.bfloat16)
    return (upper, lower)


def adamw(weight, first_mom, second, grad_in, factor, step_num, step_rate):
    clipped = grad_in * factor
    first_new = beta_one * first_mom + (1 - beta_one) * clipped
    second_new = beta_two * second + (1 - beta_two) * clipped * clipped
    fix_one = 1 - beta_one**step_num
    fix_two = 1 - beta_two**step_num
    weight_new = weight - step_rate * (
        first_new / fix_one / (jnp.sqrt(second_new / fix_two) + adam_eps) + decay_rate * weight
    )
    return (first_new, second_new, weight_new)


def local(
    query_feats,
    feature_mask,
    query_task,
    target_class,
    target_mask,
    memory_feats,
    memory_task,
    memory_mask,
    anneal,
    w_qkv,
    w_out,
    w_heads,
    w_small,
    m_qkv,
    m_out,
    m_heads,
    m_small,
    v_qkv,
    v_out,
    v_heads,
    v_small,
):
    high = lax.Precision.HIGHEST
    head_size = D // H
    full_qkv, full_out, full_heads, full_small = (
        lax.all_gather(w_qkv, "mem", axis=0, tiled=True),
        lax.all_gather(w_out, "mem", axis=0, tiled=True),
        lax.all_gather(w_heads, "mem", axis=0, tiled=True),
        lax.all_gather(w_small, "mem", axis=0, tiled=True),
    )
    emb_table = full_small[:D]
    emb_bias = full_small[D : 2 * D]
    gain_in = full_small[2 * D : 3 * D]
    gain_out = full_small[3 * D : 4 * D]
    score_coef = full_small[4 * D : 4 * D + H] * head_size ** (-0.5)
    qkv_low = full_qkv.reshape(D, 3 * D).astype(jnp.bfloat16)
    out_low = full_out.reshape(D, D).astype(jnp.bfloat16)
    heads_low = full_heads.reshape(D, C + F).astype(jnp.bfloat16)
    mem_hidden = embed(memory_feats, emb_table, emb_bias)
    mem_normed = (standard(mem_hidden)[0] * gain_in).astype(jnp.bfloat16)
    mem_kv = jnp.dot(mem_normed, qkv_low[:, D:], preferred_element_type=jnp.float32).astype(
        jnp.bfloat16
    )
    all_kv = lax.all_gather(mem_kv, "mem", axis=0, tiled=True)
    memory_rows = all_kv.shape[0]
    block_keys = math.gcd(memory_rows, 512)
    num_blocks = memory_rows // block_keys
    key_rows = all_kv[:, :D].reshape(num_blocks, block_keys, H, head_size)
    value_rows = all_kv[:, D:].reshape(num_blocks, block_keys, H, head_size)
    task_blocks = memory_task.reshape(num_blocks, block_keys)
    live_blocks = memory_mask.reshape(num_blocks, block_keys)
    key_blocks = (key_rows, value_rows, task_blocks, live_blocks)
    kept_input = query_feats * (1 - feature_mask).astype(jnp.float32)
    hidden_in = embed(kept_input, emb_table, emb_bias)
    query_normed = (standard(hidden_in)[0] * gain_in).astype(jnp.bfloat16)
    queries = (
        jnp.dot(query_normed, qkv_low[:, :D], preferred_element_type=jnp.float32)
        .astype(jnp.bfloat16)
        .reshape(-1, H, head_size)
    )
    num_rows = queries.shape[0]

    def allowed_of(task_row, live_row):
        return ((query_task[:, None] == task_row[None, :]) & (live_row[None, :] > 0))[None]

    def scores_of(key_block, allowed):
        raw_scores = jnp.einsum(
            "qhd,khd->hqk", queries, key_block, preferred_element_type=jnp.float32
        )
        return (
            raw_scores,
            jnp.where(allowed, score_coef[:, None, None] * raw_scores, masked_score),
        )

    def stats_step(state_in, block_data):
        row_top, row_sum = state_in
        key_block, value_block, task_row, live_row = block_data
        allowed = allowed_of(task_row, live_row)
        scores = scores_of(key_block, allowed)[1]
        new_top = jnp.maximum(row_top, jnp.max(scores, -1))
        shifted = jnp.where(allowed, jnp.exp(scores - new_top[..., None]), 0.0)
        return ((new_top, row_sum * jnp.exp(row_top - new_top) + jnp.sum(shifted, -1)), None)

    start_state = (
        jnp.full((H, num_rows), masked_score, jnp.float32),
        jnp.zeros((H, num_rows), jnp.float32),
    )
    (row_top, row_sum), unused = lax.scan(stats_step, start_state, key_blocks)

    def probs_of(scores, allowed):
        return jnp.where(allowed, jnp.exp(scores - row_top[..., None]), 0.0) / row_sum[..., None]

    def value_step(accum, block_data):
        key_block, value_block, task_row, live_row = block_data
        allowed = allowed_of(task_row, live_row)
        probs_low = probs_of(scores_of(key_block, allowed)[1], allowed).astype(jnp.bfloat16)
        return (
            accum
            + jnp.einsum(
                "hqk,khd->qhd", probs_low, value_block, preferred_element_type=jnp.float32
            ),
            None,
        )

    attn_sum, unused = lax.scan(
        value_step, jnp.zeros((num_rows, H, head_size), jnp.float32), key_blocks
    )
    attended = attn_sum.reshape(num_rows, D).astype(jnp.bfloat16)
    residual = hidden_in + jnp.dot(attended, out_low, preferred_element_type=jnp.float32)
    final_normed = (standard(residual)[0] * gain_out).astype(jnp.bfloat16)
    head_out = jnp.dot(final_normed, heads_low, preferred_element_type=jnp.float32)
    logits = head_out[:, :C]
    recon_err = head_out[:, C:] - query_feats
    label_mask = target_mask.astype(jnp.float32)
    feat_mask = feature_mask.astype(jnp.float32)
    onehot_class = jax.nn.one_hot(target_class, C, dtype=jnp.float32)
    picked = jnp.sum(logits * onehot_class, -1)
    sum_target, sum_recon, count_target, count_recon = lax.psum(
        (
            jnp.sum(label_mask * (jax.nn.logsumexp(logits, -1) - picked)),
            jnp.sum(feat_mask * recon_err**2),
            jnp.sum(label_mask),
            jnp.sum(feat_mask),
        ),
        "mem",
    )
    count_target = jnp.maximum(count_target, 1.0)
    count_recon = jnp.maximum(count_recon, 1.0)
    weight_a = anneal[0]
    loss_value = weight_a * sum_target / count_target + (1 - weight_a) * sum_recon / count_recon
    grad_logits = (
        weight_a / count_target * label_mask[:, None] * (jax.nn.softmax(logits, -1) - onehot_class)
    )
    grad_recon = (1 - weight_a) / count_recon * feat_mask * 2.0 * recon_err
    grad_head_out = jnp.concatenate([grad_logits, grad_recon], 1).astype(jnp.bfloat16)
    grad_heads = jnp.dot(final_normed.T, grad_head_out, preferred_element_type=jnp.float32)
    grad_final = jnp.dot(grad_head_out, heads_low.T, preferred_element_type=jnp.float32)
    grad_resid, grad_gain_out = norm_back(grad_final, residual, gain_out)
    grad_branch = grad_resid.astype(jnp.bfloat16)
    grad_wout = jnp.dot(attended.T, grad_branch, preferred_element_type=jnp.float32)
    grad_attn = (
        jnp.dot(grad_branch, out_low.T, preferred_element_type=jnp.float32)
        .astype(jnp.bfloat16)
        .reshape(num_rows, H, head_size)
    )
    row_delta = jnp.sum(
        grad_attn.astype(jnp.float32)
        * attended.reshape(num_rows, H, head_size).astype(jnp.float32),
        -1,
    ).T

    def back_step(state_in, block_data):
        key_block, value_block, task_row, live_row = block_data
        allowed = allowed_of(task_row, live_row)
        raw_scores, scores = scores_of(key_block, allowed)
        soft_probs = probs_of(scores, allowed)
        grad_probs = jnp.einsum(
            "qhd,khd->hqk", grad_attn, value_block, preferred_element_type=jnp.float32
        )
        grad_scores = (soft_probs * (grad_probs - row_delta[..., None])).astype(jnp.bfloat16)
        grad_beta = jnp.sum(grad_scores.astype(jnp.float32) * raw_scores, (1, 2))
        grad_query = jnp.einsum(
            "hqk,khd->qhd", grad_scores, key_block, preferred_element_type=jnp.float32
        )
        grad_key = (
            jnp.einsum("hqk,qhd->khd", grad_scores, queries, preferred_element_type=jnp.float32)
            * score_coef[None, :, None]
        )
        grad_value = jnp.einsum(
            "hqk,qhd->khd",
            soft_probs.astype(jnp.bfloat16),
            grad_attn,
            preferred_element_type=jnp.float32,
        )
        block_rows = key_block.shape[0]
        grad_kv = jnp.concatenate(
            [grad_key.reshape(block_rows, D), grad_value.reshape(block_rows, D)], 1
        )
        return ((state_in[0] + grad_query, state_in[1] + grad_beta), grad_kv)

    init_state = (jnp.zeros((num_rows, H, head_size), jnp.float32), jnp.zeros((H,), jnp.float32))
    (grad_q_sum, grad_beta_sum), kv_parts = lax.scan(back_step, init_state, key_blocks)
    kv_grad = lax.psum_scatter(
        kv_parts.reshape(memory_rows, 2 * D), "mem", scatter_dimension=0, tiled=True
    )
    grad_q_low = (grad_q_sum * score_coef[None, :, None]).reshape(num_rows, D).astype(jnp.bfloat16)
    grad_wq = jnp.dot(query_normed.T, grad_q_low, preferred_element_type=jnp.float32)
    grad_qn = jnp.dot(grad_q_low, qkv_low[:, :D].T, preferred_element_type=jnp.float32)
    grad_in_q, gain_in_q = norm_back(grad_qn, hidden_in, gain_in)
    grad_hidden = grad_resid + grad_in_q
    kv_upper, kv_lower = split_pair(kv_grad)
    grad_wkv = jnp.dot(mem_normed.T, kv_upper, preferred_element_type=jnp.float32) + jnp.dot(
        mem_normed.T, kv_lower, preferred_element_type=jnp.float32
    )
    grad_mn = jnp.dot(kv_upper, qkv_low[:, D:].T, preferred_element_type=jnp.float32) + jnp.dot(
        kv_lower, qkv_low[:, D:].T, preferred_element_type=jnp.float32
    )
    grad_mem, gain_in_m = norm_back(grad_mn, mem_hidden, gain_in)
    grad_table = jnp.einsum(
        "qf,qfe->fe", kept_input, grad_hidden.reshape(num_rows, F, -1), precision=high
    )
    grad_table = grad_table + jnp.einsum(
        "qf,qfe->fe", memory_feats, grad_mem.reshape(memory_feats.shape[0], F, -1), precision=high
    )
    grad_bias = jnp.sum(grad_hidden, 0) + jnp.sum(grad_mem, 0)
    small_size = full_small.shape[0]
    grad_small = jnp.concatenate(
        [
            grad_table.reshape(-1),
            grad_bias,
            gain_in_q + gain_in_m,
            grad_gain_out,
            grad_beta_sum * head_size ** (-0.5),
            jnp.zeros((small_size - 4 * D - H,), jnp.float32),
        ]
    )
    grad_qkv = jnp.concatenate([grad_wq, grad_wkv], 1).reshape(-1)
    shards = (
        lax.psum_scatter(grad_qkv, "mem", scatter_dimension=0, tiled=True),
        lax.psum_scatter(grad_wout.reshape(-1), "mem", scatter_dimension=0, tiled=True),
        lax.psum_scatter(grad_heads.reshape(-1), "mem", scatter_dimension=0, tiled=True),
        lax.psum_scatter(grad_small, "mem", scatter_dimension=0, tiled=True),
    )
    local_squares = sum((jnp.sum(piece_grad * piece_grad) for piece_grad in shards))
    grad_total = jnp.sqrt(lax.psum(local_squares, "mem"))
    factor = jnp.minimum(1.0, max_norm / (grad_total + 1e-06))
    step_num = float(STEP)
    weights_all = (w_qkv, w_out, w_heads, w_small)
    firsts = (m_qkv, m_out, m_heads, m_small)
    seconds = (v_qkv, v_out, v_heads, v_small)
    results = [
        adamw(weight, first_mom, second, grad_in, factor, step_num, step_rate)
        for weight, first_mom, second, grad_in, step_rate in zip(
            weights_all, firsts, seconds, shards, learn_rates
        )
    ]
    new_w = [entry[2] for entry in results]
    return (
        new_w[0],
        new_w[1],
        new_w[2],
        new_w[3],
        results[0][0],
        results[1][0],
        results[2][0],
        results[3][0],
        results[0][1],
        results[1][1],
        results[2][1],
        results[3][1],
        new_w[0].astype(jnp.bfloat16),
        new_w[1].astype(jnp.bfloat16),
        new_w[2].astype(jnp.bfloat16),
        new_w[3].astype(jnp.bfloat16),
        loss_value.reshape(1),
        grad_total.reshape(1),
    )


def solution(mesh):
    placed = (
        P("mem", None),
        P("mem", None),
        P("mem"),
        P("mem"),
        P("mem"),
        P("mem", None),
        P(),
        P(),
        P(),
        P("mem"),
        P("mem"),
        P("mem"),
        P("mem"),
        P("mem"),
        P("mem"),
        P("mem"),
        P("mem"),
        P("mem"),
        P("mem"),
        P("mem"),
        P("mem"),
    )
    return jax.shard_map(
        local,
        mesh=mesh,
        in_specs=placed,
        out_specs=(
            P("mem"),
            P("mem"),
            P("mem"),
            P("mem"),
            P("mem"),
            P("mem"),
            P("mem"),
            P("mem"),
            P("mem"),
            P("mem"),
            P("mem"),
            P("mem"),
            P("mem"),
            P("mem"),
            P("mem"),
            P("mem"),
            P(),
            P(),
        ),
        check_vma=False,
    )
```

profile of v0, /device:TPU:0, one launch (start us, length us, event | category | flops | bytes accessed | tf_op | source)
XLA Modules:
  0.0 763.1 jit_solution(16829456224447970304)
XLA Ops:
  9.7 42.3 %all-reduce.9 = (f32[1056]{0:T(1024)S(1)}, bf16[6144]{0:T(1024)(128)(2,1)S(1)}) all-reduce(f32[1056]{0:T(1024)S(1)} %dynamic-update-slice, f32[6144]{0:T(1024)S(1)} %dynamic-update-slice.1), channel_id=1, replica_groups=mesh['mem'=32] {'mem'}, use_global_device_ids=true, to_apply=%add | all-reduce | flops 7200 | bytes 45312
  55.3 41.3 %all_gather.16 = bf16[196608]{0:T(1024)(128)(2,1)S(1)} all-gather(bf16[6144]{0:T(1024)(128)(2,1)S(1)} %convert.24), channel_id=1, replica_groups=mesh['mem'=32] {'mem'}, dimensions={0}, use_global_device_ids=true | all-gather | bytes 405504 | tf_op jit(solution)/shard_map/all_gather | solution.py:91
  101.4 37.2 %all_gather.18 = bf16[65536]{0:T(1024)(128)(2,1)S(1)} all-gather(bf16[2048]{0:T(1024)(128)(2,1)S(1)} %convert.25), channel_id=1, replica_groups=mesh['mem'=32] {'mem'}, dimensions={0}, use_global_device_ids=true | all-gather | bytes 135168 | tf_op jit(solution)/shard_map/all_gather | solution.py:92
  142.2 8.4 %all-gather.2.cloned.1.call-done = bf16[2048,512]{1,0:T(8,128)(2,1)} async-done(((bf16[64,512]{1,0:T(8,128)(2,1)}), bf16[2048,512]{1,0:T(8,128)(2,1)}) %all-gather.2.cloned.1.call-update) | async-done | bytes 2097168 | tf_op jit(solution)/shard_map/all_gather | solution.py:109
  150.5 2.7 fusion.89
  159.5 35.7 %while.39 = (s32[]{:T(128)}, f32[8,1024]{1,0:T(8,128)S(1)}, f32[8,1024]{1,0:T(8,128)S(1)}, s32[1024]{0:T(1024)S(1)}, s32[4,512]{1,0:T(4,128)S(1)}, /*index=5*/s3...) while((s32[]{:T(128)}, f32[8,1024]{1,0:T(8,128)S(1)}, ...), condition=%wide.region_7.8_spmd.clone, body=%wide.region_4.7_spmd.clone.sunk | while | flops 303079936 | bytes 36353224 | solution.py:153
  160.0 4.1 fusion.140
  164.1 4.3 select_reduce_fusion.3
  168.9 4.1 fusion.140
  173.0 4.3 select_reduce_fusion.3
  177.8 4.1 fusion.140
  182.0 4.3 select_reduce_fusion.3
  186.8 4.1 fusion.140
  190.9 4.3 select_reduce_fusion.3
  195.3 33.3 %while.40 = (s32[]{:T(128)}, f32[1024,8,32]{0,2,1:T(8,128)S(1)}, bf16[4,512,8,32]{1,3,2,0:T(8,128)(2,1)}, s32[1024]{0:T(1024)S(1)}, s32[4,512]{1,0:T(4,128)S(1)}...) while((s32[]{:T(128)}, f32[1024,8,32]{0,2,1:T(8,128)S(1)}, ...), condition=%wide.region_9.10_spmd.clone, body=%wide.region_8.9_spmd.clone.sunk | while | flops 563610112 | bytes 4274870 | solution.py:170
  196.3 7.7 %fusion.145 = f32[1024,8,32]{0,2,1:T(8,128)S(1)} fusion(bf16[1024,8,32]{0,2,1:T(8,128)(2,1)S(1)} %get-tuple-element.853, f32[8,1024]{1,0:T(8,128)S(1)} %get-tuple-element.855, f32[8,1024]{1,0:T(8,128)S(1)} %get-tuple-element.854, f32[8]{0:T(128)S(1)} %get-tuple-element.851, pred[1024,512]{0,1:T(8,128)(4,1)S(1)} %compare_and_fusion.7, ...), kind=kOutput, calls=%fused_computation.28.clone.1 | convolution fusion | flops 562561024 | bytes 3737120 | tf_op jit(solution)/shard_map/while/body/eval_jaxpr/hqk,khd->qhd/dot_general | solution.py:164
  204.5 7.7 %fusion.145 = f32[1024,8,32]{0,2,1:T(8,128)S(1)} fusion(bf16[1024,8,32]{0,2,1:T(8,128)(2,1)S(1)} %get-tuple-element.853, f32[8,1024]{1,0:T(8,128)S(1)} %get-tuple-element.855, f32[8,1024]{1,0:T(8,128)S(1)} %get-tuple-element.854, f32[8]{0:T(128)S(1)} %get-tuple-element.851, pred[1024,512]{0,1:T(8,128)(4,1)S(1)} %compare_and_fusion.7, ...), kind=kOutput, calls=%fused_computation.28.clone.1 | convolution fusion | flops 562561024 | bytes 3737120 | tf_op jit(solution)/shard_map/while/body/eval_jaxpr/hqk,khd->qhd/dot_general | solution.py:164
  212.7 7.7 %fusion.145 = f32[1024,8,32]{0,2,1:T(8,128)S(1)} fusion(bf16[1024,8,32]{0,2,1:T(8,128)(2,1)S(1)} %get-tuple-element.853, f32[8,1024]{1,0:T(8,128)S(1)} %get-tuple-element.855, f32[8,1024]{1,0:T(8,128)S(1)} %get-tuple-element.854, f32[8]{0:T(128)S(1)} %get-tuple-element.851, pred[1024,512]{0,1:T(8,128)(4,1)S(1)} %compare_and_fusion.7, ...), kind=kOutput, calls=%fused_computation.28.clone.1 | convolution fusion | flops 562561024 | bytes 3737120 | tf_op jit(solution)/shard_map/while/body/eval_jaxpr/hqk,khd->qhd/dot_general | solution.py:164
  220.9 7.7 %fusion.145 = f32[1024,8,32]{0,2,1:T(8,128)S(1)} fusion(bf16[1024,8,32]{0,2,1:T(8,128)(2,1)S(1)} %get-tuple-element.853, f32[8,1024]{1,0:T(8,128)S(1)} %get-tuple-element.855, f32[8,1024]{1,0:T(8,128)S(1)} %get-tuple-element.854, f32[8]{0:T(128)S(1)} %get-tuple-element.851, pred[1024,512]{0,1:T(8,128)(4,1)S(1)} %compare_and_fusion.7, ...), kind=kOutput, calls=%fused_computation.28.clone.1 | convolution fusion | flops 562561024 | bytes 3737120 | tf_op jit(solution)/shard_map/while/body/eval_jaxpr/hqk,khd->qhd/dot_general | solution.py:164
  234.2 38.8 %all-reduce.8 = (f32[]{:T(128)}, f32[]{:T(128)}) all-reduce(f32[]{:T(128)} %get-tuple-element.440, f32[]{:T(128)} %get-tuple-element.442), channel_id=1, replica_groups=mesh['mem'=32] {'mem'}, use_global_device_ids=true, to_apply=%region_17.18 | all-reduce | flops 2 | bytes 16 | tf_op jit(solution)/shard_map/psum | solution.py:183
  278.5 150.5 %while.41 = (s32[]{:T(128)}, f32[1024,8,32]{0,2,1:T(8,128)}, f32[8]{0:T(128)}, f32[4,512,512]{2,1,0:T(8,128)}, bf16[4,512,8,32]{1,3,2,0:T(8,128)(2,1)}, /*index=...) while((s32[]{:T(128)}, f32[1024,8,32]{0,2,1:T(8,128)}, ...), condition=%wide.region_23.24_spmd.clone, body=%wide.region_21.23_spmd.clone.sunk | while | flops 1415447040 | bytes 156940240 | solution.py:247
  279.9 3.3 fusion.155
  283.3 5.7 copy-done
  289.0 6.7 fusion.159
  295.7 12.7 %fusion.156 = (f32[8]{0:T(128)S(1)}, bf16[8,1024,512]{1,2,0:T(8,128)(2,1)S(1)}) fusion(f32[8,512,1024]{2,1,0:T(8,128)} %copy-done, f32[8,1024]{1,0:T(8,128)} %get-tuple-element.906, bf16[1024,8,32]{0,2,1:T(8,128)(2,1)} %get-tuple-element.905, bf16[4,512,8,32]{1,3,2,0:T(8,128)(2,1)} %get-tuple-element.904, s32[]{:T(128)S(6)} %copy.149, ...), kind=kOutput, calls=%fused_computation.47.clone.1 | convolution fusion | flops 314572800 | bytes 26574916 | tf_op jit(solution)/shard_map/while/body/eval_jaxpr/qhd,khd->hqk/dot_general | solution.py:222
  308.4 2.6 convolution_multiply_fusion.2
  311.0 3.5 fusion.157
  317.2 3.3 fusion.155
  320.5 5.7 copy-done
  326.2 6.7 fusion.159
  332.9 12.7 %fusion.156 = (f32[8]{0:T(128)S(1)}, bf16[8,1024,512]{1,2,0:T(8,128)(2,1)S(1)}) fusion(f32[8,512,1024]{2,1,0:T(8,128)} %copy-done, f32[8,1024]{1,0:T(8,128)} %get-tuple-element.906, bf16[1024,8,32]{0,2,1:T(8,128)(2,1)} %get-tuple-element.905, bf16[4,512,8,32]{1,3,2,0:T(8,128)(2,1)} %get-tuple-element.904, s32[]{:T(128)S(6)} %copy.149, ...), kind=kOutput, calls=%fused_computation.47.clone.1 | convolution fusion | flops 314572800 | bytes 26574916 | tf_op jit(solution)/shard_map/while/body/eval_jaxpr/qhd,khd->hqk/dot_general | solution.py:222
  345.6 2.6 convolution_multiply_fusion.2
  348.2 3.9 fusion.157
  354.8 3.3 fusion.155
  358.1 5.7 copy-done
  363.9 6.7 fusion.159
  370.5 12.7 %fusion.156 = (f32[8]{0:T(128)S(1)}, bf16[8,1024,512]{1,2,0:T(8,128)(2,1)S(1)}) fusion(f32[8,512,1024]{2,1,0:T(8,128)} %copy-done, f32[8,1024]{1,0:T(8,128)} %get-tuple-element.906, bf16[1024,8,32]{0,2,1:T(8,128)(2,1)} %get-tuple-element.905, bf16[4,512,8,32]{1,3,2,0:T(8,128)(2,1)} %get-tuple-element.904, s32[]{:T(128)S(6)} %copy.149, ...), kind=kOutput, calls=%fused_computation.47.clone.1 | convolution fusion | flops 314572800 | bytes 26574916 | tf_op jit(solution)/shard_map/while/body/eval_jaxpr/qhd,khd->hqk/dot_general | solution.py:222
  385.9 3.9 fusion.157
  392.4 3.3 fusion.155
  395.7 5.7 copy-done
  401.4 6.7 fusion.159
  408.1 12.7 %fusion.156 = (f32[8]{0:T(128)S(1)}, bf16[8,1024,512]{1,2,0:T(8,128)(2,1)S(1)}) fusion(f32[8,512,1024]{2,1,0:T(8,128)} %copy-done, f32[8,1024]{1,0:T(8,128)} %get-tuple-element.906, bf16[1024,8,32]{0,2,1:T(8,128)(2,1)} %get-tuple-element.905, bf16[4,512,8,32]{1,3,2,0:T(8,128)(2,1)} %get-tuple-element.904, s32[]{:T(128)S(6)} %copy.149, ...), kind=kOutput, calls=%fused_computation.47.clone.1 | convolution fusion | flops 314572800 | bytes 26574916 | tf_op jit(solution)/shard_map/while/body/eval_jaxpr/qhd,khd->hqk/dot_general | solution.py:222
  420.8 2.6 convolution_multiply_fusion.2
  423.4 3.9 fusion.157
  442.5 128.2 %reduce-scatter.2.cloned.1.call-done = f32[64,512]{1,0:T(8,128)} async-done(((f32[2048,512]{1,0:T(8,128)}), f32[64,512]{1,0:T(8,128)}) %reduce-scatter.2.cloned.1.call-update) | async-done | bytes 131088 | tf_op jit(solution)/shard_map/reduce_scatter | solution.py:248
  577.5 37.4 %all-reduce.7 = (f32[6144]{0:T(1024)S(1)}, f32[1056]{0:T(1024)S(1)}) all-reduce(f32[6144]{0:T(1024)S(1)} %reshape.518, f32[1056]{0:T(1024)S(1)} %concatenate.15), channel_id=5, replica_groups=mesh['mem'=32] {'mem'}, use_global_device_ids=true, to_apply=%region_29.30.clone | all-reduce | flops 7200 | bytes 57600
  616.3 86.9 %all-reduce.13.cloned.1.call-done = (f32[196608]{0:T(1024)}, f32[65536]{0:T(1024)}) async-done(((f32[196608]{0:T(1024)}, f32[65536]{0:T(1024)}), (f32[196608]{0:T(1024)}, f32[65536]{0:T(1024)})) %all-reduce.13.cloned.1.call-update) | async-done | bytes 1048592
  708.4 39.5 %all-reduce.6 = (f32[]{:T(128)}, f32[]{:T(128)}, f32[]{:T(128)}) all-reduce(f32[]{:T(128)S(6)} %add.225, f32[]{:T(128)} %get-tuple-element.441, f32[]{:T(128)} %get-tuple-element.439), channel_id=1, replica_groups=mesh['mem'=32] {'mem'}, use_global_device_ids=true, to_apply=%region_42.43 | all-reduce | flops 3 | bytes 24 | tf_op jit(solution)/shard_map/psum | solution.py:290
  (324 shorter events, 74.0 us)
Async XLA Ops:
  7.2 152.2 %copy-start.16 = (s32[1024]{0:T(1024)S(1)}, s32[1024]{0:T(1024)}, u32[]{:S(2)}) copy-start(s32[1024]{0:T(1024)} %param.29) | copy-start | bytes 12292
  7.2 143.3 %all-gather.2.cloned.1.call-start = ((), (), s32[]{:S(2)}) async-start(), calls=%async_computation.1 | async-start | bytes 2162688 | tf_op jit(solution)/shard_map/all_gather | solution.py:109
  52.6 106.8 %copy-start.33 = (f32[256]{0:T(256)}, f32[256]{0:T(256)S(1)}, u32[]{:S(2)}) copy-start(f32[256]{0:T(256)S(1)} %get-tuple-element.553) | copy-start | bytes 3076
  52.6 106.8 %copy-start.35 = (f32[256]{0:T(256)}, f32[256]{0:T(256)S(1)}, u32[]{:S(2)}) copy-start(f32[256]{0:T(256)S(1)} %get-tuple-element.554) | copy-start | bytes 3076
  52.6 106.8 %copy-start.37 = (f32[256]{0:T(256)}, f32[256]{0:T(256)S(1)}, u32[]{:S(2)}) copy-start(f32[256]{0:T(256)S(1)} %get-tuple-element.555) | copy-start | bytes 3076
  52.7 106.8 %copy-start.27 = (f32[8,32]{1,0:T(8,128)}, f32[8,32]{1,0:T(8,128)S(1)}, u32[]{:S(2)}) copy-start(f32[8,32]{1,0:T(8,128)S(1)} %add.204) | copy-start | bytes 3076
  52.8 106.7 %copy-start.28 = (f32[8,32]{1,0:T(8,128)}, f32[8,32]{1,0:T(8,128)S(1)}, u32[]{:S(2)}) copy-start(f32[8,32]{1,0:T(8,128)S(1)} %mul.534) | copy-start | bytes 3076
  53.6 85.7 %copy-start.46 = (f32[64]{0:T(128)}, f32[64]{0:T(128)S(1)}, u32[]{:S(2)}) copy-start(f32[64]{0:T(128)S(1)} %broadcast_multiply_fusion.9) | copy-start | bytes 772
  54.5 105.0 %copy-start.50 = (f32[64]{0:T(128)}, f32[64]{0:T(128)S(1)}, u32[]{:S(2)}) copy-start(f32[64]{0:T(128)S(1)} %add_rsqrt_fusion.2) | copy-start | bytes 772
  55.3 86.6 %copy-start.11 = (f32[64,256]{1,0:T(8,128)}, f32[64,256]{1,0:T(8,128)S(1)}, u32[]{:S(2)}) copy-start(f32[64,256]{1,0:T(8,128)S(1)} %copy.69) | copy-start | bytes 196612
  96.9 56.3 %copy-start.6 = (bf16[256,768]{1,0:T(8,128)(2,1)}, bf16[256,768]{1,0:T(8,128)(2,1)S(1)}, u32[]{:S(2)}) copy-start(bf16[256,768]{1,0:T(8,128)(2,1)S(1)} %convert_element_type.124) | copy-start | bytes 1179652
  97.8 472.9 %reduce-scatter.2.cloned.1.call-start = ((), (), s32[]{:S(2)}) async-start(), calls=%async_computation.2 | async-start | bytes 4325376 | tf_op jit(solution)/shard_map/reduce_scatter | solution.py:248
  159.4 35.8 %copy-start.14 = (f32[1024,8,32]{0,2,1:T(8,128)S(1)}, f32[1024,8,32]{0,2,1:T(8,128)}, u32[]{:S(2)}) copy-start(f32[1024,8,32]{0,2,1:T(8,128)} %custom-call.2) | copy-start | bytes 3145732
  195.3 36.3 %copy-start.43 = (f32[256]{0:T(256)S(1)}, f32[256]{0:T(256)}, u32[]{:S(2)}) copy-start(f32[256]{0:T(256)} %get-tuple-element.552) | copy-start | bytes 3076
  195.3 37.3 %copy-start.19 = (bf16[256,24]{1,0:T(8,128)(2,1)S(1)}, bf16[256,24]{1,0:T(8,128)(2,1)}, u32[]{:S(2)}) copy-start(bf16[256,24]{1,0:T(8,128)(2,1)} %convert_element_type.135) | copy-start | bytes 36868
  195.3 37.5 %copy-start.21 = (f32[1024,8]{0,1:T(8,128)S(1)}, f32[1024,8]{0,1:T(8,128)}, u32[]{:S(2)}) copy-start(f32[1024,8]{0,1:T(8,128)} %param.27) | copy-start | bytes 98308
  195.3 37.5 %copy-start.22 = (s32[1024,8]{0,1:T(8,128)S(1)}, s32[1024,8]{0,1:T(8,128)}, u32[]{:S(2)}) copy-start(s32[1024,8]{0,1:T(8,128)} %param.28) | copy-start | bytes 98308
  195.3 38.2 %copy-start.44 = (s32[1024]{0:T(1024)S(1)}, s32[1024]{0:T(1024)}, u32[]{:S(2)}) copy-start(s32[1024]{0:T(1024)} %param.30) | copy-start | bytes 12292
  195.3 38.2 %copy-start.45 = (s32[1024]{0:T(1024)S(1)}, s32[1024]{0:T(1024)}, u32[]{:S(2)}) copy-start(s32[1024]{0:T(1024)} %param.31) | copy-start | bytes 12292
  229.7 44.6 %copy-start.29 = (f32[8]{0:T(128)}, f32[8]{0:T(128)S(1)}, u32[]{:S(2)}) copy-start(f32[8]{0:T(128)S(1)} %get-tuple-element.934) | copy-start | bytes 100
  229.7 48.8 %copy-start.8 = (f32[8,1024]{1,0:T(8,128)}, f32[8,1024]{1,0:T(8,128)S(1)}, u32[]{:S(2)}) copy-start(f32[8,1024]{1,0:T(8,128)S(1)} %get-tuple-element.919) | copy-start | bytes 98308
  229.7 48.8 %copy-start.17 = (f32[8,1024]{1,0:T(8,128)}, f32[8,1024]{1,0:T(8,128)S(1)}, u32[]{:S(2)}) copy-start(f32[8,1024]{1,0:T(8,128)S(1)} %get-tuple-element.928) | copy-start | bytes 98308
  229.7 48.8 %copy-start.23 = (s32[4,512]{1,0:T(4,128)}, s32[4,512]{1,0:T(4,128)S(1)}, u32[]{:S(2)}) copy-start(s32[4,512]{1,0:T(4,128)S(1)} %get-tuple-element.932) | copy-start | bytes 24580
  231.0 47.5 %copy-start.2 = (bf16[1024,8,32]{0,2,1:T(8,128)(2,1)}, bf16[1024,8,32]{0,2,1:T(8,128)(2,1)S(1)}, u32[]{:S(2)}) copy-start(bf16[1024,8,32]{0,2,1:T(8,128)(2,1)S(1)} %convert_element_type.128) | copy-start | bytes 1572868
  278.5 151.6 %copy-start.25 = (f32[1024]{0:T(1024)S(1)}, f32[1024]{0:T(1024)}, u32[]{:S(2)}) copy-start(f32[1024]{0:T(1024)} %copy-done.24) | copy-start | bytes 12292
  278.5 152.7 %copy-start.4 = (bf16[1024,256]{0,1:T(8,128)(2,1)S(1)}, bf16[1024,256]{0,1:T(8,128)(2,1)}, u32[]{:S(2)}) copy-start(bf16[1024,256]{0,1:T(8,128)(2,1)} %copy-done.3) | copy-start | bytes 1572868
  278.5 157.9 %copy-start.7 = (bf16[256,768]{1,0:T(8,128)(2,1)S(1)}, bf16[256,768]{1,0:T(8,128)(2,1)}, u32[]{:S(2)}) copy-start(bf16[256,768]{1,0:T(8,128)(2,1)} %copy-done.6) | copy-start | bytes 1179652
  429.0 142.8 %copy-start.12 = (f32[64,256]{1,0:T(8,128)S(1)}, f32[64,256]{1,0:T(8,128)}, u32[]{:S(2)}) copy-start(f32[64,256]{1,0:T(8,128)} %copy-done.11) | copy-start | bytes 196612
  429.0 142.8 %copy-start.34 = (f32[256]{0:T(256)S(1)}, f32[256]{0:T(256)}, u32[]{:S(2)}) copy-start(f32[256]{0:T(256)} %copy-done.33) | copy-start | bytes 3076
  429.0 142.8 %copy-start.36 = (f32[256]{0:T(256)S(1)}, f32[256]{0:T(256)}, u32[]{:S(2)}) copy-start(f32[256]{0:T(256)} %copy-done.35) | copy-start | bytes 3076
  429.0 142.8 %copy-start.38 = (f32[256]{0:T(256)S(1)}, f32[256]{0:T(256)}, u32[]{:S(2)}) copy-start(f32[256]{0:T(256)} %copy-done.37) | copy-start | bytes 3076
  429.0 142.8 %copy-start.47 = (f32[64]{0:T(128)S(1)}, f32[64]{0:T(128)}, u32[]{:S(2)}) copy-start(f32[64]{0:T(128)} %copy-done.46) | copy-start | bytes 772
  429.1 142.8 %copy-start.51 = (f32[64]{0:T(128)S(1)}, f32[64]{0:T(128)}, u32[]{:S(2)}) copy-start(f32[64]{0:T(128)} %copy-done.50) | copy-start | bytes 772
  429.1 147.9 %copy-start.39 = (f32[64,8]{0,1:T(8,128)S(1)}, f32[64,8]{0,1:T(8,128)}, u32[]{:S(2)}) copy-start(f32[64,8]{0,1:T(8,128)} %param.32) | copy-start | bytes 6148
  429.1 148.4 %copy-start.54 = (f32[256]{0:T(256)S(1)}, f32[256]{0:T(256)}, u32[]{:S(2)}) copy-start(f32[256]{0:T(256)} %get-tuple-element.427) | copy-start | bytes 3076
  429.1 321.0 %copy-start.32 = (f32[6144]{0:T(1024)S(1)}, f32[6144]{0:T(1024)}, u32[]{:S(2)}) copy-start(f32[6144]{0:T(1024)} %param.36) | copy-start | bytes 73732
  429.1 321.0 %copy-start.41 = (f32[6144]{0:T(1024)S(1)}, f32[6144]{0:T(1024)}, u32[]{:S(2)}) copy-start(f32[6144]{0:T(1024)} %param.40) | copy-start | bytes 73732
  429.1 321.0 %copy-start.42 = (f32[6144]{0:T(1024)S(1)}, f32[6144]{0:T(1024)}, u32[]{:S(2)}) copy-start(f32[6144]{0:T(1024)} %param.44) | copy-start | bytes 73732
  429.1 322.3 %copy-start.40 = (f32[2048]{0:T(1024)S(1)}, f32[2048]{0:T(1024)}, u32[]{:S(2)}) copy-start(f32[2048]{0:T(1024)} %param.37) | copy-start | bytes 24580
  429.1 322.3 %copy-start.52 = (f32[2048]{0:T(1024)S(1)}, f32[2048]{0:T(1024)}, u32[]{:S(2)}) copy-start(f32[2048]{0:T(1024)} %param.41) | copy-start | bytes 24580
  429.2 322.3 %copy-start.53 = (f32[2048]{0:T(1024)S(1)}, f32[2048]{0:T(1024)}, u32[]{:S(2)}) copy-start(f32[2048]{0:T(1024)} %param.45) | copy-start | bytes 24580
  429.2 323.6 %copy-start.55 = (f32[192]{0:T(256)S(1)}, f32[192]{0:T(256)}, u32[]{:S(2)}) copy-start(f32[192]{0:T(256)} %param.38) | copy-start | bytes 2308
  429.2 323.6 %copy-start.56 = (f32[192]{0:T(256)S(1)}, f32[192]{0:T(256)}, u32[]{:S(2)}) copy-start(f32[192]{0:T(256)} %param.42) | copy-start | bytes 2308
  429.2 323.6 %copy-start.57 = (f32[192]{0:T(256)S(1)}, f32[192]{0:T(256)}, u32[]{:S(2)}) copy-start(f32[192]{0:T(256)} %param.46) | copy-start | bytes 2308
  429.2 324.3 %copy-start.58 = (f32[33]{0:T(128)S(1)}, f32[33]{0:T(128)}, u32[]{:S(2)}) copy-start(f32[33]{0:T(128)} %param.39) | copy-start | bytes 400
  429.2 324.3 %copy-start.59 = (f32[33]{0:T(128)S(1)}, f32[33]{0:T(128)}, u32[]{:S(2)}) copy-start(f32[33]{0:T(128)} %param.43) | copy-start | bytes 400
  429.2 324.3 %copy-start.60 = (f32[33]{0:T(128)S(1)}, f32[33]{0:T(128)}, u32[]{:S(2)}) copy-start(f32[33]{0:T(128)} %param.47) | copy-start | bytes 400
  429.3 273.9 %all-reduce.13.cloned.1.call-start = ((), (), s32[]{:S(2)}) async-start(), calls=%async_computation.3 | async-start | bytes 2097152
  (34 other events, 338.3 us)
Sparse Core Ops, SparseCore 0:
  97.9 52.5 all-gather.1
  429.4 141.2 reduce-scatter.1
  576.9 126.2 all-reduce.12
where the time goes:
time: 773 us; the launch traced here: 763 us
  blocking collectives  236 us (31%)
  waiting for transfers between devices  224 us (29%)
  matrix products  180 us (23%)
  local copies, waits for them, and re-layouts  49.9 us (6%)
  other arithmetic  47.9 us (6%)
  between operations  24 us (3%)
    reduce_scatter x1, waiting for transfers between devices, local(): lax.psum_scatter(kv_parts.reshape(memory_rows, 2 * D), 'mem', scatter_dim...  128 us
    unnamed x4, waiting for transfers between devices  86.9 us
    unnamed x2, blocking collectives  79.7 us
    dot_general x4, matrix products, back_step(): jnp.einsum('qhd,khd->hqk', grad_attn, value_block, preferred_element_type...  50.8 us
    all_gather x1, blocking collectives, local(): lax.all_gather(w_qkv, 'mem', axis=0, tiled=True)  41.3 us
    psum x1, blocking collectives, local(): grad_total = jnp.sqrt(lax.psum(local_squares, 'mem'))  39.5 us
    psum x1, blocking collectives, local(): lax.psum((jnp.sum(label_mask * (jax.nn.logsumexp(logits, -1) - picked)),...  38.8 us
    all_gather x1, blocking collectives, local(): lax.all_gather(w_out, 'mem', axis=0, tiled=True)  37.2 us
  transfers between devices with their start and end apart: 3, of which 3 were waited for; matrix products, arithmetic and copies ran while one was open for 3% of the time, Pallas kernels for 0%

commit v1 on v0

--- a/solution.py
+++ b/solution.py
@@ -287,7 +287,7 @@
         lax.psum_scatter(grad_small, "mem", scatter_dimension=0, tiled=True),
     )
     local_squares = sum((jnp.sum(piece_grad * piece_grad) for piece_grad in shards))
-    grad_total = jnp.sqrt(lax.psum(local_squares, "mem"))
+    grad_total = jnp.sqrt(jnp.sum(lax.all_gather(local_squares, "mem"), axis=0))
     factor = jnp.minimum(1.0, max_norm / (grad_total + 1e-06))
     step_num = float(STEP)
     weights_all = (w_qkv, w_out, w_heads, w_small)

time: 773 us -> 774 us (level)
    psum x1 -> x0, blocking collectives: 39.5 us -> none  [local(): grad_total = jnp.sqrt(lax.psum(local_squares, 'mem'))]
    unnamed x2 -> x3, blocking collectives: 79.7 us -> 119 us
where the time goes in v1:
time: 774 us; the launch traced here: 764 us
  blocking collectives  236 us (30%)
  waiting for transfers between devices  224 us (29%)
  matrix products  180 us (23%)
  local copies, waits for them, and re-layouts  50 us (6%)
  other arithmetic  48.5 us (6%)
  between operations  24 us (3%)
    reduce_scatter x1, waiting for transfers between devices, local(): lax.psum_scatter(kv_parts.reshape(memory_rows, 2 * D), 'mem', scatter_dim...  128 us
    unnamed x3, blocking collectives  119 us
    unnamed x4, waiting for transfers between devices  86.9 us
    dot_general x4, matrix products, back_step(): jnp.einsum('qhd,khd->hqk', grad_attn, value_block, preferred_element_type...  50.8 us
    all_gather x1, blocking collectives, local(): lax.all_gather(w_qkv, 'mem', axis=0, tiled=True)  41.3 us
    psum x1, blocking collectives, local(): lax.psum((jnp.sum(label_mask * (jax.nn.logsumexp(logits, -1) - picked)),...  38.8 us
    all_gather x1, blocking collectives, local(): lax.all_gather(w_out, 'mem', axis=0, tiled=True)  37.2 us
    dot_general x4, matrix products, value_step(): jnp.einsum('hqk,khd->qhd', probs_low, value_block, preferred_element_type...  30.9 us
  transfers between devices with their start and end apart: 3, of which 3 were waited for; matrix products, arithmetic and copies ran while one was open for 3% of the time, Pallas kernels for 0%

profile of v1, /device:TPU:0, one launch (start us, length us, event | category | flops | bytes accessed | tf_op | source)
XLA Modules:
  0.0 763.8 jit_solution(8605791139226970495)
XLA Ops:
  9.7 42.3 %all-reduce.10 = (f32[1056]{0:T(1024)S(1)}, bf16[6144]{0:T(1024)(128)(2,1)S(1)}) all-reduce(f32[1056]{0:T(1024)S(1)} %dynamic-update-slice, f32[6144]{0:T(1024)S(1)} %dynamic-update-slice.1), channel_id=1, replica_groups=mesh['mem'=32] {'mem'}, use_global_device_ids=true, to_apply=%add | all-reduce | flops 7200 | bytes 45312
  55.3 41.3 %all_gather.22 = bf16[196608]{0:T(1024)(128)(2,1)S(1)} all-gather(bf16[6144]{0:T(1024)(128)(2,1)S(1)} %convert.24), channel_id=1, replica_groups=mesh['mem'=32] {'mem'}, dimensions={0}, use_global_device_ids=true | all-gather | bytes 405504 | tf_op jit(solution)/shard_map/all_gather | solution.py:91
  101.4 37.2 %all_gather.24 = bf16[65536]{0:T(1024)(128)(2,1)S(1)} all-gather(bf16[2048]{0:T(1024)(128)(2,1)S(1)} %convert.25), channel_id=1, replica_groups=mesh['mem'=32] {'mem'}, dimensions={0}, use_global_device_ids=true | all-gather | bytes 135168 | tf_op jit(solution)/shard_map/all_gather | solution.py:92
  142.2 8.4 %all-gather.2.cloned.1.call-done = bf16[2048,512]{1,0:T(8,128)(2,1)} async-done(((bf16[64,512]{1,0:T(8,128)(2,1)}), bf16[2048,512]{1,0:T(8,128)(2,1)}) %all-gather.2.cloned.1.call-update) | async-done | bytes 2097168 | tf_op jit(solution)/shard_map/all_gather | solution.py:109
  150.5 2.7 fusion.89
  159.5 35.7 %while.39 = (s32[]{:T(128)}, f32[8,1024]{1,0:T(8,128)S(1)}, f32[8,1024]{1,0:T(8,128)S(1)}, s32[1024]{0:T(1024)S(1)}, s32[4,512]{1,0:T(4,128)S(1)}, /*index=5*/s3...) while((s32[]{:T(128)}, f32[8,1024]{1,0:T(8,128)S(1)}, ...), condition=%wide.region_7.8_spmd.clone, body=%wide.region_4.7_spmd.clone.sunk | while | flops 303079936 | bytes 36353224 | solution.py:153
  160.0 4.1 fusion.140
  164.1 4.3 select_reduce_fusion.3
  168.9 4.1 fusion.140
  173.0 4.3 select_reduce_fusion.3
  177.8 4.1 fusion.140
  182.0 4.3 select_reduce_fusion.3
  186.8 4.1 fusion.140
  190.9 4.3 select_reduce_fusion.3
  195.3 33.3 %while.40 = (s32[]{:T(128)}, f32[1024,8,32]{0,2,1:T(8,128)S(1)}, bf16[4,512,8,32]{1,3,2,0:T(8,128)(2,1)}, s32[1024]{0:T(1024)S(1)}, s32[4,512]{1,0:T(4,128)S(1)}...) while((s32[]{:T(128)}, f32[1024,8,32]{0,2,1:T(8,128)S(1)}, ...), condition=%wide.region_9.10_spmd.clone, body=%wide.region_8.9_spmd.clone.sunk | while | flops 563610112 | bytes 4274870 | solution.py:170
  196.3 7.7 %fusion.145 = f32[1024,8,32]{0,2,1:T(8,128)S(1)} fusion(bf16[1024,8,32]{0,2,1:T(8,128)(2,1)S(1)} %get-tuple-element.853, f32[8,1024]{1,0:T(8,128)S(1)} %get-tuple-element.855, f32[8,1024]{1,0:T(8,128)S(1)} %get-tuple-element.854, f32[8]{0:T(128)S(1)} %get-tuple-element.851, pred[1024,512]{0,1:T(8,128)(4,1)S(1)} %compare_and_fusion.7, ...), kind=kOutput, calls=%fused_computation.28.clone.1 | convolution fusion | flops 562561024 | bytes 3737120 | tf_op jit(solution)/shard_map/while/body/eval_jaxpr/hqk,khd->qhd/dot_general | solution.py:164
  204.5 7.7 %fusion.145 = f32[1024,8,32]{0,2,1:T(8,128)S(1)} fusion(bf16[1024,8,32]{0,2,1:T(8,128)(2,1)S(1)} %get-tuple-element.853, f32[8,1024]{1,0:T(8,128)S(1)} %get-tuple-element.855, f32[8,1024]{1,0:T(8,128)S(1)} %get-tuple-element.854, f32[8]{0:T(128)S(1)} %get-tuple-element.851, pred[1024,512]{0,1:T(8,128)(4,1)S(1)} %compare_and_fusion.7, ...), kind=kOutput, calls=%fused_computation.28.clone.1 | convolution fusion | flops 562561024 | bytes 3737120 | tf_op jit(solution)/shard_map/while/body/eval_jaxpr/hqk,khd->qhd/dot_general | solution.py:164
  212.7 7.7 %fusion.145 = f32[1024,8,32]{0,2,1:T(8,128)S(1)} fusion(bf16[1024,8,32]{0,2,1:T(8,128)(2,1)S(1)} %get-tuple-element.853, f32[8,1024]{1,0:T(8,128)S(1)} %get-tuple-element.855, f32[8,1024]{1,0:T(8,128)S(1)} %get-tuple-element.854, f32[8]{0:T(128)S(1)} %get-tuple-element.851, pred[1024,512]{0,1:T(8,128)(4,1)S(1)} %compare_and_fusion.7, ...), kind=kOutput, calls=%fused_computation.28.clone.1 | convolution fusion | flops 562561024 | bytes 3737120 | tf_op jit(solution)/shard_map/while/body/eval_jaxpr/hqk,khd->qhd/dot_general | solution.py:164
  220.9 7.7 %fusion.145 = f32[1024,8,32]{0,2,1:T(8,128)S(1)} fusion(bf16[1024,8,32]{0,2,1:T(8,128)(2,1)S(1)} %get-tuple-element.853, f32[8,1024]{1,0:T(8,128)S(1)} %get-tuple-element.855, f32[8,1024]{1,0:T(8,128)S(1)} %get-tuple-element.854, f32[8]{0:T(128)S(1)} %get-tuple-element.851, pred[1024,512]{0,1:T(8,128)(4,1)S(1)} %compare_and_fusion.7, ...), kind=kOutput, calls=%fused_computation.28.clone.1 | convolution fusion | flops 562561024 | bytes 3737120 | tf_op jit(solution)/shard_map/while/body/eval_jaxpr/hqk,khd->qhd/dot_general | solution.py:164
  234.2 38.8 %all-reduce.9 = (f32[]{:T(128)}, f32[]{:T(128)}) all-reduce(f32[]{:T(128)} %get-tuple-element.440, f32[]{:T(128)} %get-tuple-element.442), channel_id=1, replica_groups=mesh['mem'=32] {'mem'}, use_global_device_ids=true, to_apply=%region_17.18 | all-reduce | flops 2 | bytes 16 | tf_op jit(solution)/shard_map/psum | solution.py:183
  278.5 150.5 %while.41 = (s32[]{:T(128)}, f32[1024,8,32]{0,2,1:T(8,128)}, f32[8]{0:T(128)}, f32[4,512,512]{2,1,0:T(8,128)}, bf16[4,512,8,32]{1,3,2,0:T(8,128)(2,1)}, /*index=...) while((s32[]{:T(128)}, f32[1024,8,32]{0,2,1:T(8,128)}, ...), condition=%wide.region_23.24_spmd.clone, body=%wide.region_21.23_spmd.clone.sunk | while | flops 1415447040 | bytes 156940240 | solution.py:247
  279.9 3.3 fusion.155
  283.3 5.7 copy-done
  289.0 6.7 fusion.159
  295.7 12.7 %fusion.156 = (f32[8]{0:T(128)S(1)}, bf16[8,1024,512]{1,2,0:T(8,128)(2,1)S(1)}) fusion(f32[8,512,1024]{2,1,0:T(8,128)} %copy-done, f32[8,1024]{1,0:T(8,128)} %get-tuple-element.906, bf16[1024,8,32]{0,2,1:T(8,128)(2,1)} %get-tuple-element.905, bf16[4,512,8,32]{1,3,2,0:T(8,128)(2,1)} %get-tuple-element.904, s32[]{:T(128)S(6)} %copy.150, ...), kind=kOutput, calls=%fused_computation.47.clone.1 | convolution fusion | flops 314572800 | bytes 26574916 | tf_op jit(solution)/shard_map/while/body/eval_jaxpr/qhd,khd->hqk/dot_general | solution.py:222
  308.4 2.6 convolution_multiply_fusion.2
  311.0 3.5 fusion.157
  317.2 3.3 fusion.155
  320.5 5.7 copy-done
  326.2 6.7 fusion.159
  332.9 12.7 %fusion.156 = (f32[8]{0:T(128)S(1)}, bf16[8,1024,512]{1,2,0:T(8,128)(2,1)S(1)}) fusion(f32[8,512,1024]{2,1,0:T(8,128)} %copy-done, f32[8,1024]{1,0:T(8,128)} %get-tuple-element.906, bf16[1024,8,32]{0,2,1:T(8,128)(2,1)} %get-tuple-element.905, bf16[4,512,8,32]{1,3,2,0:T(8,128)(2,1)} %get-tuple-element.904, s32[]{:T(128)S(6)} %copy.150, ...), kind=kOutput, calls=%fused_computation.47.clone.1 | convolution fusion | flops 314572800 | bytes 26574916 | tf_op jit(solution)/shard_map/while/body/eval_jaxpr/qhd,khd->hqk/dot_general | solution.py:222
  345.6 2.6 convolution_multiply_fusion.2
  348.2 3.9 fusion.157
  354.8 3.3 fusion.155
  358.1 5.7 copy-done
  363.9 6.7 fusion.159
  370.5 12.7 %fusion.156 = (f32[8]{0:T(128)S(1)}, bf16[8,1024,512]{1,2,0:T(8,128)(2,1)S(1)}) fusion(f32[8,512,1024]{2,1,0:T(8,128)} %copy-done, f32[8,1024]{1,0:T(8,128)} %get-tuple-element.906, bf16[1024,8,32]{0,2,1:T(8,128)(2,1)} %get-tuple-element.905, bf16[4,512,8,32]{1,3,2,0:T(8,128)(2,1)} %get-tuple-element.904, s32[]{:T(128)S(6)} %copy.150, ...), kind=kOutput, calls=%fused_computation.47.clone.1 | convolution fusion | flops 314572800 | bytes 26574916 | tf_op jit(solution)/shard_map/while/body/eval_jaxpr/qhd,khd->hqk/dot_general | solution.py:222
  385.9 3.9 fusion.157
  392.4 3.3 fusion.155
  395.7 5.7 copy-done
  401.4 6.7 fusion.159
  408.1 12.7 %fusion.156 = (f32[8]{0:T(128)S(1)}, bf16[8,1024,512]{1,2,0:T(8,128)(2,1)S(1)}) fusion(f32[8,512,1024]{2,1,0:T(8,128)} %copy-done, f32[8,1024]{1,0:T(8,128)} %get-tuple-element.906, bf16[1024,8,32]{0,2,1:T(8,128)(2,1)} %get-tuple-element.905, bf16[4,512,8,32]{1,3,2,0:T(8,128)(2,1)} %get-tuple-element.904, s32[]{:T(128)S(6)} %copy.150, ...), kind=kOutput, calls=%fused_computation.47.clone.1 | convolution fusion | flops 314572800 | bytes 26574916 | tf_op jit(solution)/shard_map/while/body/eval_jaxpr/qhd,khd->hqk/dot_general | solution.py:222
  420.8 2.6 convolution_multiply_fusion.2
  423.4 3.9 fusion.157
  442.5 128.2 %reduce-scatter.2.cloned.1.call-done = f32[64,512]{1,0:T(8,128)} async-done(((f32[2048,512]{1,0:T(8,128)}), f32[64,512]{1,0:T(8,128)}) %reduce-scatter.2.cloned.1.call-update) | async-done | bytes 131088 | tf_op jit(solution)/shard_map/reduce_scatter | solution.py:248
  577.5 37.4 %all-reduce.8 = (f32[6144]{0:T(1024)S(1)}, f32[1056]{0:T(1024)S(1)}) all-reduce(f32[6144]{0:T(1024)S(1)} %reshape.518, f32[1056]{0:T(1024)S(1)} %concatenate.15), channel_id=5, replica_groups=mesh['mem'=32] {'mem'}, use_global_device_ids=true, to_apply=%region_29.30.clone | all-reduce | flops 7200 | bytes 57600
  616.3 86.9 %all-reduce.14.cloned.1.call-done = (f32[196608]{0:T(1024)}, f32[65536]{0:T(1024)}) async-done(((f32[196608]{0:T(1024)}, f32[65536]{0:T(1024)}), (f32[196608]{0:T(1024)}, f32[65536]{0:T(1024)})) %all-reduce.14.cloned.1.call-update) | async-done | bytes 1048592
  708.6 39.4 %all-reduce.7 = (f32[32]{0:T(128)S(1)}, f32[]{:T(128)}, f32[]{:T(128)}) all-reduce(f32[32]{0:T(128)S(1)} %dynamic-update-slice.2, f32[]{:T(128)} %get-tuple-element.441, f32[]{:T(128)} %get-tuple-element.439), channel_id=1, replica_groups=mesh['mem'=32] {'mem'}, use_global_device_ids=true, to_apply=%add.2 | all-reduce | flops 34 | bytes 272
  (327 shorter events, 74.7 us)
Async XLA Ops:
  7.2 152.2 %copy-start.16 = (s32[1024]{0:T(1024)S(1)}, s32[1024]{0:T(1024)}, u32[]{:S(2)}) copy-start(s32[1024]{0:T(1024)} %param.29) | copy-start | bytes 12292
  7.2 143.3 %all-gather.2.cloned.1.call-start = ((), (), s32[]{:S(2)}) async-start(), calls=%async_computation.1 | async-start | bytes 2162688 | tf_op jit(solution)/shard_map/all_gather | solution.py:109
  52.6 106.8 %copy-start.33 = (f32[256]{0:T(256)}, f32[256]{0:T(256)S(1)}, u32[]{:S(2)}) copy-start(f32[256]{0:T(256)S(1)} %get-tuple-element.553) | copy-start | bytes 3076
  52.6 106.8 %copy-start.35 = (f32[256]{0:T(256)}, f32[256]{0:T(256)S(1)}, u32[]{:S(2)}) copy-start(f32[256]{0:T(256)S(1)} %get-tuple-element.554) | copy-start | bytes 3076
  52.6 106.8 %copy-start.37 = (f32[256]{0:T(256)}, f32[256]{0:T(256)S(1)}, u32[]{:S(2)}) copy-start(f32[256]{0:T(256)S(1)} %get-tuple-element.555) | copy-start | bytes 3076
  52.7 106.8 %copy-start.27 = (f32[8,32]{1,0:T(8,128)}, f32[8,32]{1,0:T(8,128)S(1)}, u32[]{:S(2)}) copy-start(f32[8,32]{1,0:T(8,128)S(1)} %add.202) | copy-start | bytes 3076
  52.8 106.7 %copy-start.28 = (f32[8,32]{1,0:T(8,128)}, f32[8,32]{1,0:T(8,128)S(1)}, u32[]{:S(2)}) copy-start(f32[8,32]{1,0:T(8,128)S(1)} %mul.534) | copy-start | bytes 3076
  53.6 85.7 %copy-start.46 = (f32[64]{0:T(128)}, f32[64]{0:T(128)S(1)}, u32[]{:S(2)}) copy-start(f32[64]{0:T(128)S(1)} %broadcast_multiply_fusion.9) | copy-start | bytes 772
  54.5 105.0 %copy-start.50 = (f32[64]{0:T(128)}, f32[64]{0:T(128)S(1)}, u32[]{:S(2)}) copy-start(f32[64]{0:T(128)S(1)} %add_rsqrt_fusion.2) | copy-start | bytes 772
  55.3 86.6 %copy-start.11 = (f32[64,256]{1,0:T(8,128)}, f32[64,256]{1,0:T(8,128)S(1)}, u32[]{:S(2)}) copy-start(f32[64,256]{1,0:T(8,128)S(1)} %copy.69) | copy-start | bytes 196612
  96.9 56.3 %copy-start.6 = (bf16[256,768]{1,0:T(8,128)(2,1)}, bf16[256,768]{1,0:T(8,128)(2,1)S(1)}, u32[]{:S(2)}) copy-start(bf16[256,768]{1,0:T(8,128)(2,1)S(1)} %convert_element_type.124) | copy-start | bytes 1179652
  97.8 472.9 %reduce-scatter.2.cloned.1.call-start = ((), (), s32[]{:S(2)}) async-start(), calls=%async_computation.2 | async-start | bytes 4325376 | tf_op jit(solution)/shard_map/reduce_scatter | solution.py:248
  159.4 35.8 %copy-start.14 = (f32[1024,8,32]{0,2,1:T(8,128)S(1)}, f32[1024,8,32]{0,2,1:T(8,128)}, u32[]{:S(2)}) copy-start(f32[1024,8,32]{0,2,1:T(8,128)} %custom-call.2) | copy-start | bytes 3145732
  195.3 36.3 %copy-start.43 = (f32[256]{0:T(256)S(1)}, f32[256]{0:T(256)}, u32[]{:S(2)}) copy-start(f32[256]{0:T(256)} %get-tuple-element.552) | copy-start | bytes 3076
  195.3 37.3 %copy-start.19 = (bf16[256,24]{1,0:T(8,128)(2,1)S(1)}, bf16[256,24]{1,0:T(8,128)(2,1)}, u32[]{:S(2)}) copy-start(bf16[256,24]{1,0:T(8,128)(2,1)} %convert_element_type.135) | copy-start | bytes 36868
  195.3 37.5 %copy-start.21 = (f32[1024,8]{0,1:T(8,128)S(1)}, f32[1024,8]{0,1:T(8,128)}, u32[]{:S(2)}) copy-start(f32[1024,8]{0,1:T(8,128)} %param.27) | copy-start | bytes 98308
  195.3 37.5 %copy-start.22 = (s32[1024,8]{0,1:T(8,128)S(1)}, s32[1024,8]{0,1:T(8,128)}, u32[]{:S(2)}) copy-start(s32[1024,8]{0,1:T(8,128)} %param.28) | copy-start | bytes 98308
  195.3 38.2 %copy-start.44 = (s32[1024]{0:T(1024)S(1)}, s32[1024]{0:T(1024)}, u32[]{:S(2)}) copy-start(s32[1024]{0:T(1024)} %param.30) | copy-start | bytes 12292
  195.3 38.2 %copy-start.45 = (s32[1024]{0:T(1024)S(1)}, s32[1024]{0:T(1024)}, u32[]{:S(2)}) copy-start(s32[1024]{0:T(1024)} %param.31) | copy-start | bytes 12292
  229.7 44.6 %copy-start.29 = (f32[8]{0:T(128)}, f32[8]{0:T(128)S(1)}, u32[]{:S(2)}) copy-start(f32[8]{0:T(128)S(1)} %get-tuple-element.934) | copy-start | bytes 100
  229.7 48.8 %copy-start.8 = (f32[8,1024]{1,0:T(8,128)}, f32[8,1024]{1,0:T(8,128)S(1)}, u32[]{:S(2)}) copy-start(f32[8,1024]{1,0:T(8,128)S(1)} %get-tuple-element.919) | copy-start | bytes 98308
  229.7 48.8 %copy-start.17 = (f32[8,1024]{1,0:T(8,128)}, f32[8,1024]{1,0:T(8,128)S(1)}, u32[]{:S(2)}) copy-start(f32[8,1024]{1,0:T(8,128)S(1)} %get-tuple-element.928) | copy-start | bytes 98308
  229.7 48.8 %copy-start.23 = (s32[4,512]{1,0:T(4,128)}, s32[4,512]{1,0:T(4,128)S(1)}, u32[]{:S(2)}) copy-start(s32[4,512]{1,0:T(4,128)S(1)} %get-tuple-element.932) | copy-start | bytes 24580
  231.0 47.5 %copy-start.2 = (bf16[1024,8,32]{0,2,1:T(8,128)(2,1)}, bf16[1024,8,32]{0,2,1:T(8,128)(2,1)S(1)}, u32[]{:S(2)}) copy-start(bf16[1024,8,32]{0,2,1:T(8,128)(2,1)S(1)} %convert_element_type.128) | copy-start | bytes 1572868
  278.5 151.6 %copy-start.25 = (f32[1024]{0:T(1024)S(1)}, f32[1024]{0:T(1024)}, u32[]{:S(2)}) copy-start(f32[1024]{0:T(1024)} %copy-done.24) | copy-start | bytes 12292
  278.5 152.7 %copy-start.4 = (bf16[1024,256]{0,1:T(8,128)(2,1)S(1)}, bf16[1024,256]{0,1:T(8,128)(2,1)}, u32[]{:S(2)}) copy-start(bf16[1024,256]{0,1:T(8,128)(2,1)} %copy-done.3) | copy-start | bytes 1572868
  278.5 157.9 %copy-start.7 = (bf16[256,768]{1,0:T(8,128)(2,1)S(1)}, bf16[256,768]{1,0:T(8,128)(2,1)}, u32[]{:S(2)}) copy-start(bf16[256,768]{1,0:T(8,128)(2,1)} %copy-done.6) | copy-start | bytes 1179652
  429.0 142.8 %copy-start.12 = (f32[64,256]{1,0:T(8,128)S(1)}, f32[64,256]{1,0:T(8,128)}, u32[]{:S(2)}) copy-start(f32[64,256]{1,0:T(8,128)} %copy-done.11) | copy-start | bytes 196612
  429.0 142.8 %copy-start.34 = (f32[256]{0:T(256)S(1)}, f32[256]{0:T(256)}, u32[]{:S(2)}) copy-start(f32[256]{0:T(256)} %copy-done.33) | copy-start | bytes 3076
  429.0 142.8 %copy-start.36 = (f32[256]{0:T(256)S(1)}, f32[256]{0:T(256)}, u32[]{:S(2)}) copy-start(f32[256]{0:T(256)} %copy-done.35) | copy-start | bytes 3076
  429.0 142.8 %copy-start.38 = (f32[256]{0:T(256)S(1)}, f32[256]{0:T(256)}, u32[]{:S(2)}) copy-start(f32[256]{0:T(256)} %copy-done.37) | copy-start | bytes 3076
  429.0 142.8 %copy-start.47 = (f32[64]{0:T(128)S(1)}, f32[64]{0:T(128)}, u32[]{:S(2)}) copy-start(f32[64]{0:T(128)} %copy-done.46) | copy-start | bytes 772
  429.1 142.8 %copy-start.51 = (f32[64]{0:T(128)S(1)}, f32[64]{0:T(128)}, u32[]{:S(2)}) copy-start(f32[64]{0:T(128)} %copy-done.50) | copy-start | bytes 772
  429.1 147.9 %copy-start.39 = (f32[64,8]{0,1:T(8,128)S(1)}, f32[64,8]{0,1:T(8,128)}, u32[]{:S(2)}) copy-start(f32[64,8]{0,1:T(8,128)} %param.32) | copy-start | bytes 6148
  429.1 148.4 %copy-start.54 = (f32[256]{0:T(256)S(1)}, f32[256]{0:T(256)}, u32[]{:S(2)}) copy-start(f32[256]{0:T(256)} %get-tuple-element.427) | copy-start | bytes 3076
  429.1 321.6 %copy-start.32 = (f32[6144]{0:T(1024)S(1)}, f32[6144]{0:T(1024)}, u32[]{:S(2)}) copy-start(f32[6144]{0:T(1024)} %param.36) | copy-start | bytes 73732
  429.1 321.6 %copy-start.41 = (f32[6144]{0:T(1024)S(1)}, f32[6144]{0:T(1024)}, u32[]{:S(2)}) copy-start(f32[6144]{0:T(1024)} %param.40) | copy-start | bytes 73732
  429.1 321.6 %copy-start.42 = (f32[6144]{0:T(1024)S(1)}, f32[6144]{0:T(1024)}, u32[]{:S(2)}) copy-start(f32[6144]{0:T(1024)} %param.44) | copy-start | bytes 73732
  429.1 323.0 %copy-start.40 = (f32[2048]{0:T(1024)S(1)}, f32[2048]{0:T(1024)}, u32[]{:S(2)}) copy-start(f32[2048]{0:T(1024)} %param.37) | copy-start | bytes 24580
  429.1 323.0 %copy-start.52 = (f32[2048]{0:T(1024)S(1)}, f32[2048]{0:T(1024)}, u32[]{:S(2)}) copy-start(f32[2048]{0:T(1024)} %param.41) | copy-start | bytes 24580
  429.2 323.0 %copy-start.53 = (f32[2048]{0:T(1024)S(1)}, f32[2048]{0:T(1024)}, u32[]{:S(2)}) copy-start(f32[2048]{0:T(1024)} %param.45) | copy-start | bytes 24580
  429.2 324.3 %copy-start.55 = (f32[192]{0:T(256)S(1)}, f32[192]{0:T(256)}, u32[]{:S(2)}) copy-start(f32[192]{0:T(256)} %param.38) | copy-start | bytes 2308
  429.2 324.3 %copy-start.56 = (f32[192]{0:T(256)S(1)}, f32[192]{0:T(256)}, u32[]{:S(2)}) copy-start(f32[192]{0:T(256)} %param.42) | copy-start | bytes 2308
  429.2 324.3 %copy-start.57 = (f32[192]{0:T(256)S(1)}, f32[192]{0:T(256)}, u32[]{:S(2)}) copy-start(f32[192]{0:T(256)} %param.46) | copy-start | bytes 2308
  429.2 325.0 %copy-start.58 = (f32[33]{0:T(128)S(1)}, f32[33]{0:T(128)}, u32[]{:S(2)}) copy-start(f32[33]{0:T(128)} %param.39) | copy-start | bytes 400
  429.2 325.0 %copy-start.59 = (f32[33]{0:T(128)S(1)}, f32[33]{0:T(128)}, u32[]{:S(2)}) copy-start(f32[33]{0:T(128)} %param.43) | copy-start | bytes 400
  429.2 324.9 %copy-start.60 = (f32[33]{0:T(128)S(1)}, f32[33]{0:T(128)}, u32[]{:S(2)}) copy-start(f32[33]{0:T(128)} %param.47) | copy-start | bytes 400
  429.3 273.9 %all-reduce.14.cloned.1.call-start = ((), (), s32[]{:S(2)}) async-start(), calls=%async_computation.3 | async-start | bytes 2097152
  (34 other events, 338.3 us)
Sparse Core Ops, SparseCore 0:
  97.9 52.5 all-gather.1
  429.4 141.2 reduce-scatter.1
  576.9 126.2 all-reduce.13
